TPU v7x, 32 devices: a whole 2x2x4 slice. The times are simulated.
32 devices in a mesh: seq: 4 (over y, x), batch: 8 (over z, core).
Axes of the slice: x: 2, y: 2, z: 4, core: 2. Of those that a mesh axis runs over, the one named last changes fastest.
Arguments:
- tokens: bfloat16 [8, 2048, 768], P('batch', 'seq'), may hold values from -6 to 6
- segment_ids: int32 [8, 2048], P('batch', 'seq'), may hold values from 0 to 10, as said below
- span_starts: int32 [8, 32], P('batch', 'seq'), may hold values from 0 to 1, as said below
- first_gain: float32 [768], replicated, may hold values from 0.5 to 1.5
- first_shift: float32 [768], replicated, may hold values from -3 to 3
- second_gain: float32 [768], replicated, may hold values from 0.5 to 1.5
- second_shift: float32 [768], replicated, may hold values from -3 to 3
- input_weight: bfloat16 [768, 2304], replicated, may hold values from -0.21875 to 0.21875
- input_bias: float32 [2304], replicated, may hold values from -3 to 3
- feature_freq: float32 [64, 64], replicated, may hold values from -4 to 4
- feature_weight: float32 [12, 64], replicated, may hold values from 0.5 to 2
- output_weight: bfloat16 [768, 768], replicated, may hold values from -1.75 to 1.75
- output_bias: float32 [768], replicated, may hold values from -3 to 3
- up_weight: bfloat16 [768, 3072], replicated, may hold values from -0.21875 to 0.21875
- up_bias: float32 [3072], replicated, may hold values from -3 to 3
- down_weight: bfloat16 [3072, 768], replicated, may hold values from -0.109375 to 0.109375
- down_bias: float32 [768], replicated, may hold values from -3 to 3
- cotangent: bfloat16 [8, 2048, 768], P('batch', 'seq'), may hold values from -6 to 6
Outputs:
- result: bfloat16 [8, 2048, 768], P('batch', 'seq')
- tokens_grad: bfloat16 [8, 2048, 768], P('batch', 'seq')
- first_gain_grad: float32 [768], replicated
- first_shift_grad: float32 [768], replicated
- second_gain_grad: float32 [768], replicated
- second_shift_grad: float32 [768], replicated
- input_weight_grad: float32 [768, 2304], replicated
- input_bias_grad: float32 [2304], replicated
- feature_weight_grad: float32 [12, 64], replicated
- output_weight_grad: float32 [768, 768], replicated
- output_bias_grad: float32 [768], replicated
- up_weight_grad: float32 [768, 3072], replicated
- up_bias_grad: float32 [3072], replicated
- down_weight_grad: float32 [3072, 768], replicated
- down_bias_grad: float32 [768], replicated
Inputs may be any that keep to these rules, and one draw needn't show every extreme that they name: `segment_ids`: along each sequence the ids start at 0 and rise by one exactly where a document begins; every sequence holds the same number of documents, and documents run across span and device boundaries. `span_starts`: 1 exactly where the span's first token has another segment id than the token before it, and for each sequence's first span.
All inputs are finite; a program needn't handle non-finite values.
Results may differ from a plain program's by a relative error of at most 0.012.
The roundings to bfloat16 on the way count: a program that leaves them out, or rounds other values in their place, can miss the bound.
Values sent between devices are 32-bit elements; how exact they have to be, the bound alone decides.
No kernel may reach another device: no remote copies, remote signals or barrier semaphores. Data moves between devices by JAX's collectives and lax.ppermute only.
A program may use at most 192 MiB of HBM per device.

v0:
```python
import math

import jax
import jax.numpy as jnp
from jax import lax
from jax.sharding import PartitionSpec as P

ROT = 16
SPAN = 64


HIGH = lax.Precision.HIGHEST
EPSILON = 1e-05
ROT_BASE = 10000.0


def carried_in(array, axis, combine, identity, reverse):
    count, place = (lax.axis_size(axis), lax.axis_index(axis))
    everything = jax.tree.map(lambda part: lax.all_gather(part, axis), array)
    start = jax.tree.map(
        lambda part, zero: jnp.broadcast_to(jnp.asarray(zero, part.dtype), part.shape),
        array,
        identity,
    )

    def lap(k, before):
        at = count - 1 - k if reverse else k
        reached = at > place if reverse else at < place
        new = combine(before, jax.tree.map(lambda part: part[at], everything))
        return jax.tree.map(lambda a, b: jnp.where(reached, a, b), new, before)

    return lax.fori_loop(0, count, lap, start)


def layer_norm(values, gain, shift):
    centre = jnp.mean(values, axis=-1, keepdims=True)
    centred = values - centre
    spread = jnp.mean(centred * centred, axis=-1, keepdims=True)
    return centred * lax.rsqrt(spread + EPSILON) * gain + shift


def cosine_table(points):
    index = jnp.arange(points, dtype=jnp.float32)
    table = jnp.cos(math.pi * (index[None, :] + 0.5) * index[:, None] / points) * math.sqrt(
        2.0 / points
    )
    return table * jnp.where(index[:, None] == 0, math.sqrt(0.5), 1.0)


def projection(feature_freq):
    points = feature_freq.shape[0]
    return jnp.dot(
        cosine_table(points).T, feature_freq, preferred_element_type=jnp.float32, precision=HIGH
    )


def angles(positions, rot_width):
    freq = ROT_BASE ** (-2.0 * jnp.arange(rot_width // 2, dtype=jnp.float32) / rot_width)
    turn = positions.astype(jnp.float32)[:, None] * freq[None, :]
    return (jnp.cos(turn), jnp.sin(turn))


def rotary(values, cosine, sine):
    half = cosine.shape[-1]
    front = values[..., :half]
    middle = values[..., half : 2 * half]
    remain = values[..., 2 * half :]
    cos_b = cosine[:, None, :]
    sin_b = sine[:, None, :]
    return jnp.concatenate(
        [front * cos_b - middle * sin_b, middle * cos_b + front * sin_b, remain], axis=-1
    )


def feature_map(values, proj, weight):
    scaled = values * math.sqrt(2.0 / values.shape[-1])
    lifted = jnp.einsum("...hd,df->...hf", scaled, proj, precision=HIGH)
    expo = lifted - 0.5 * jnp.sum(scaled * scaled, axis=-1, keepdims=True)
    return weight * jnp.exp(expo)


def exact_gelu(values):
    return jax.nn.gelu(values, approximate=False)


def combine(earlier, following):
    return (
        following[0] + following[2][:, None, None, None] * earlier[0],
        following[1] + following[2][:, None, None] * earlier[1],
        earlier[2] * following[2],
    )


def per_device(
    tokens,
    segment_ids,
    span_starts,
    first_gain,
    first_shift,
    second_gain,
    second_shift,
    input_weight,
    input_bias,
    feature_freq,
    feature_weight,
    output_weight,
    output_bias,
    up_weight,
    up_bias,
    down_weight,
    down_bias,
    cotangent,
):
    seq_count, length, model_width = tokens.shape
    head_count, feat_count = feature_weight.shape
    head_width = model_width // head_count
    blocks = length // SPAN
    row_count = seq_count * length
    f32 = jnp.float32
    b16 = jnp.bfloat16
    as_float = tokens.astype(f32)

    def norms(values, gain_one, shift_one, gain_two, shift_two):
        return (layer_norm(values, gain_one, shift_one), layer_norm(values, gain_two, shift_two))

    (first_norm, second_norm), norm_back = jax.vjp(
        norms, as_float, first_gain, first_shift, second_gain, second_shift
    )
    first_low = first_norm.astype(b16).reshape(row_count, model_width)
    second_low = second_norm.astype(b16).reshape(row_count, model_width)
    mixed = jnp.dot(first_low, input_weight, preferred_element_type=f32) + input_bias
    queries = mixed[:, :model_width].reshape(seq_count, length, head_count, head_width)
    keys = mixed[:, model_width : 2 * model_width].reshape(
        seq_count, length, head_count, head_width
    )
    value_low = (
        mixed[:, 2 * model_width :]
        .astype(b16)
        .reshape(seq_count, blocks, SPAN, head_count, head_width)
    )
    offset = lax.axis_index("seq") * length
    cosine, sine = angles(offset + jnp.arange(length), ROT)
    proj = projection(feature_freq)

    def lift(query_in, key_in, weight):
        return (
            feature_map(rotary(query_in, cosine, sine), proj, weight),
            feature_map(rotary(key_in, cosine, sine), proj, weight),
        )

    (query_phi, key_phi), feat_back = jax.vjp(lift, queries, keys, feature_weight)
    query_low = query_phi.astype(b16).reshape(seq_count, blocks, SPAN, head_count, feat_count)
    key_low = key_phi.astype(b16).reshape(seq_count, blocks, SPAN, head_count, feat_count)
    query_wide = query_low.astype(f32)
    segs = segment_ids.reshape(seq_count, blocks, SPAN)
    opened = span_starts.astype(f32)
    causal = jnp.arange(SPAN)[:, None] >= jnp.arange(SPAN)[None, :]
    pair_mask = ((segs[:, :, :, None] == segs[:, :, None, :]) & causal[None, None]).astype(f32)
    keep_first = (1.0 - opened)[:, :, None] * (segs == segs[:, :, :1]).astype(f32)
    last_doc = (segs == segs[:, :, -1:]).astype(f32)
    flow_gate = (1.0 - opened) * (segs[:, :, 0] == segs[:, :, -1]).astype(f32)
    scores = (
        jnp.einsum("bnthf,bnshf->bnhts", query_low, key_low, preferred_element_type=f32)
        * pair_mask[:, :, None]
    )
    score_low = scores.astype(b16)
    key_last = key_low * last_doc[..., None, None].astype(b16)
    local = jnp.einsum("bnshf,bnshd->bnhfd", key_last, value_low, preferred_element_type=f32)
    local_norm = jnp.sum(key_last.astype(f32), axis=2)
    closed = 1.0 - flow_gate
    lower_tri = (jnp.arange(blocks)[:, None] > jnp.arange(blocks)[None, :]).astype(f32)
    upper_tri = (jnp.arange(blocks)[None, :] >= jnp.arange(blocks)[:, None]).astype(f32)
    before = jnp.einsum("cj,bj->bc", lower_tri, closed, precision=HIGH)
    through = before + closed
    total_closed = through[:, -1]
    reach_mat = lower_tri[None] * (before[:, :, None] == through[:, None, :]).astype(f32)
    entry_gate = (before == 0.0).astype(f32)
    tail_gate = (total_closed[:, None] == through).astype(f32)
    whole_gate = (total_closed == 0.0).astype(f32)
    summary = (
        jnp.einsum("bj,bjhfd->bhfd", tail_gate, local, precision=HIGH),
        jnp.einsum("bj,bjhf->bhf", tail_gate, local_norm, precision=HIGH),
        whole_gate,
    )
    identity = (jnp.zeros_like(summary[0]), jnp.zeros_like(summary[1]), jnp.ones_like(whole_gate))
    carried, carried_norm, _ = carried_in(summary, "seq", combine, identity, False)
    state = (
        jnp.einsum("bcj,bjhfd->bchfd", reach_mat, local, precision=HIGH)
        + entry_gate[:, :, None, None, None] * carried[:, None]
    )
    state_norm = (
        jnp.einsum("bcj,bjhf->bchf", reach_mat, local_norm, precision=HIGH)
        + entry_gate[:, :, None, None] * carried_norm[:, None]
    )
    state_low = state.astype(b16)
    inside = jnp.einsum("bnhts,bnshd->bnthd", score_low, value_low, preferred_element_type=f32)
    outside = (
        jnp.einsum("bnthf,bnhfd->bnthd", query_low, state_low, preferred_element_type=f32)
        * keep_first[..., None, None]
    )
    numer = inside + outside
    denom = (
        jnp.swapaxes(jnp.sum(scores, axis=-1), 2, 3)
        + jnp.einsum("bnthf,bnhf->bnth", query_wide, state_norm, precision=HIGH)
        * keep_first[..., None]
    )
    attended = numer / denom[..., None]
    attn_low = attended.astype(b16).reshape(row_count, model_width)
    attn_out = jnp.dot(attn_low, output_weight, preferred_element_type=f32) + output_bias
    hidden = jnp.dot(second_low, up_weight, preferred_element_type=f32) + up_bias
    active, gelu_back = jax.vjp(exact_gelu, hidden)
    active_low = active.astype(b16)
    mlp_out = jnp.dot(active_low, down_weight, preferred_element_type=f32) + down_bias
    result = (as_float.reshape(row_count, model_width) + attn_out + mlp_out).astype(b16)
    grad_rows = cotangent.reshape(row_count, model_width)
    bias_total = jnp.sum(grad_rows.astype(f32), axis=0)
    down_weight_grad = jnp.einsum("tf,td->fd", active_low, grad_rows, preferred_element_type=f32)
    output_weight_grad = jnp.einsum("ti,td->id", attn_low, grad_rows, preferred_element_type=f32)
    d_active = jnp.einsum("td,fd->tf", grad_rows, down_weight, preferred_element_type=f32)
    (d_hidden_f,) = gelu_back(d_active)
    d_hidden = d_hidden_f.astype(b16)
    up_weight_grad = jnp.einsum("td,tf->df", second_low, d_hidden, preferred_element_type=f32)
    up_bias_grad = jnp.sum(d_hidden.astype(f32), axis=0)
    d_second = jnp.einsum("tf,df->td", d_hidden, up_weight, preferred_element_type=f32)
    d_attended = jnp.einsum("te,de->td", grad_rows, output_weight, preferred_element_type=f32)
    d_attended = d_attended.reshape(seq_count, blocks, SPAN, head_count, head_width)
    d_numer = (d_attended / denom[..., None]).astype(b16)
    d_denom = -jnp.sum(d_attended * attended, axis=-1) / denom
    d_score_part = jnp.einsum("bnthd,bnshd->bnhts", d_numer, value_low, preferred_element_type=f32)
    d_value = jnp.einsum("bnhts,bnthd->bnshd", score_low, d_numer, preferred_element_type=f32)
    d_scores = (
        (d_score_part + jnp.swapaxes(d_denom, 2, 3)[..., None]) * pair_mask[:, :, None]
    ).astype(b16)
    d_query = jnp.einsum("bnhts,bnshf->bnthf", d_scores, key_low, preferred_element_type=f32)
    d_key = jnp.einsum("bnhts,bnthf->bnshf", d_scores, query_low, preferred_element_type=f32)
    query_keep = query_low * keep_first[..., None, None].astype(b16)
    here = jnp.einsum("bnthf,bnthd->bnhfd", query_keep, d_numer, preferred_element_type=f32)
    here_norm = jnp.einsum(
        "bnth,bnthf->bnhf", d_denom * keep_first[..., None], query_wide, precision=HIGH
    )
    d_query = d_query + keep_first[..., None, None] * (
        jnp.einsum("bnthd,bnhfd->bnthf", d_numer, state_low, preferred_element_type=f32)
        + d_denom[..., None] * state_norm[:, :, None]
    )
    ahead_mat = upper_tri[None] * (before[:, :, None] == before[:, None, :]).astype(f32)
    leaving = (total_closed[:, None] == before).astype(f32)
    back_summary = (
        jnp.einsum("bj,bjhfd->bhfd", ahead_mat[:, 0], here, precision=HIGH),
        jnp.einsum("bj,bjhf->bhf", ahead_mat[:, 0], here_norm, precision=HIGH),
        whole_gate,
    )
    later_grad, later_norm_grad, _ = carried_in(back_summary, "seq", combine, identity, True)
    d_state = (
        jnp.einsum("bcj,bjhfd->bchfd", ahead_mat, here, precision=HIGH)
        + leaving[:, :, None, None, None] * later_grad[:, None]
    )
    d_state_norm = (
        jnp.einsum("bcj,bjhf->bchf", ahead_mat, here_norm, precision=HIGH)
        + leaving[:, :, None, None] * later_norm_grad[:, None]
    )
    d_local = jnp.concatenate([d_state[:, 1:], later_grad[:, None]], axis=1).astype(b16)
    d_local_norm = jnp.concatenate([d_state_norm[:, 1:], later_norm_grad[:, None]], axis=1)
    d_key = d_key + last_doc[..., None, None] * (
        jnp.einsum("bnshd,bnhfd->bnshf", value_low, d_local, preferred_element_type=f32)
        + d_local_norm[:, :, None]
    )
    d_value = d_value + last_doc[..., None, None] * jnp.einsum(
        "bnshf,bnhfd->bnshd", key_low, d_local, preferred_element_type=f32
    )
    d_queries, d_keys, feature_weight_grad = feat_back(
        (
            d_query.reshape(seq_count, length, head_count, feat_count),
            d_key.reshape(seq_count, length, head_count, feat_count),
        )
    )
    d_mixed = jnp.concatenate(
        [
            d_queries.reshape(row_count, model_width),
            d_keys.reshape(row_count, model_width),
            d_value.reshape(row_count, model_width),
        ],
        axis=1,
    ).astype(b16)
    input_weight_grad = jnp.einsum("td,te->de", first_low, d_mixed, preferred_element_type=f32)
    input_bias_grad = jnp.sum(d_mixed.astype(f32), axis=0)
    d_first = jnp.einsum("te,de->td", d_mixed, input_weight, preferred_element_type=f32)
    d_inputs, first_gain_grad, first_shift_grad, second_gain_grad, second_shift_grad = norm_back(
        (
            d_first.reshape(seq_count, length, model_width),
            d_second.reshape(seq_count, length, model_width),
        )
    )
    tokens_grad = (cotangent.astype(f32) + d_inputs).astype(b16)
    small = lax.psum(
        (
            first_gain_grad,
            first_shift_grad,
            second_gain_grad,
            second_shift_grad,
            input_bias_grad,
            feature_weight_grad,
            bias_total,
            up_bias_grad,
        ),
        ("seq", "batch"),
    )
    matrices = (input_weight_grad, output_weight_grad, up_weight_grad, down_weight_grad)
    shares = (
        lax.psum_scatter(matrices[0], "batch", scatter_dimension=0, tiled=True),
        lax.psum_scatter(matrices[1], "batch", scatter_dimension=0, tiled=True),
        lax.psum_scatter(matrices[2], "batch", scatter_dimension=0, tiled=True),
        lax.psum_scatter(matrices[3], "batch", scatter_dimension=0, tiled=True),
    )
    shares = lax.psum((shares[0], shares[1], shares[2], shares[3]), "seq")
    summed = (
        lax.all_gather(shares[0], "batch", axis=0, tiled=True),
        lax.all_gather(shares[1], "batch", axis=0, tiled=True),
        lax.all_gather(shares[2], "batch", axis=0, tiled=True),
        lax.all_gather(shares[3], "batch", axis=0, tiled=True),
    )
    return (
        result.reshape(seq_count, length, model_width),
        tokens_grad,
        small[0],
        small[1],
        small[2],
        small[3],
        summed[0],
        small[4],
        small[5],
        summed[1],
        small[6],
        summed[2],
        small[7],
        summed[3],
        small[6],
    )


def solution(mesh):
    in_specs = (
        P("batch", "seq", None),
        P("batch", "seq"),
        P("batch", "seq"),
        P(),
        P(),
        P(),
        P(),
        P(),
        P(),
        P(),
        P(),
        P(),
        P(),
        P(),
        P(),
        P(),
        P(),
        P("batch", "seq", None),
    )
    out_specs = (
        P("batch", "seq", None),
        P("batch", "seq", None),
        P(),
        P(),
        P(),
        P(),
        P(),
        P(),
        P(),
        P(),
        P(),
        P(),
        P(),
        P(),
        P(),
    )
    return jax.shard_map(
        per_device, mesh=mesh, in_specs=in_specs, out_specs=out_specs, check_vma=False
    )
```

profile of v0, /device:TPU:1, one launch (start us, length us, event | category | flops | bytes accessed | tf_op | source)
XLA Modules:
  0.0 1003.7 jit_solution(12177849052037369909)
XLA Ops:
  18.0 3.0 copy.124
  21.0 3.0 copy.122
  31.3 3.6 multiply_convert_fusion.3
  34.9 3.2 reshape.1211
  38.1 3.2 reshape.1215
  57.5 9.8 all-reduce.6
  70.3 3.5 fusion.103
  73.8 3.3 reshape.1221
  77.1 3.8 reshape.1273
  80.9 3.2 reshape.1209
  89.9 6.1 all-gather.4
  96.1 3.0 copy.126
  99.1 2.8 fusion.63
  101.9 3.8 fusion.23
  105.7 14.8 %all-gather = f32[48,64,64]{2,1,0:T(8,128)} all-gather(f32[12,64,64]{2,1,0:T(8,128)S(1)} %bitcast.363), channel_id=2, replica_groups=mesh['seq'=4,'batch'=8] {'seq'}, dimensions={0}, use_global_device_ids=true | all-gather | bytes 983040 | tf_op jit(solution)/shard_map/all_gather | solution.py:19
  120.5 20.3 %while.34 = (s32[]{:T(128)}, f32[1,12,64,64]{3,2,1,0:T(8,128)}, f32[1,12,64]{2,1,0:T(8,128)S(1)}, s32[]{:T(128)}, f32[4,1,12,64,64]{4,3,2,1,0:T(8,128)}, /*index...) while((s32[]{:T(128)}, f32[1,12,64,64]{3,2,1,0:T(8,128)}, ...), condition=%wide.region_6.7_spmd.clone, body=%wide.region_5.6_spmd.clone.sunk | while | flops 199684 | bytes 599191 | solution.py:32
  128.1 2.6 fusion.236
  133.2 2.6 fusion.236
  138.3 2.6 fusion.236
  142.9 6.7 add_convert_fusion.2
  155.7 2.5 fusion.18
  160.6 3.7 reshape.1216
  164.3 3.6 fusion.101
  169.1 3.3 reshape.1220
  177.6 2.6 fusion.89
  181.2 4.3 fusion.19
  185.5 14.3 %all-gather.2 = f32[48,64,64]{2,1,0:T(8,128)} all-gather(f32[12,64,64]{2,1,0:T(8,128)S(1)} %bitcast.364), channel_id=4, replica_groups=mesh['seq'=4,'batch'=8] {'seq'}, dimensions={0}, use_global_device_ids=true | all-gather | bytes 983040 | tf_op jit(solution)/shard_map/all_gather | solution.py:19
  202.6 7.3 all-gather.5
  209.9 20.8 %while.35 = (s32[]{:T(128)}, f32[1,12,64,64]{3,2,1,0:T(8,128)}, f32[1,12,64]{2,1,0:T(8,128)S(1)}, s32[]{:T(128)}, f32[4,1,12,64,64]{4,3,2,1,0:T(8,128)}, /*index...) while((s32[]{:T(128)}, f32[1,12,64,64]{3,2,1,0:T(8,128)}, ...), condition=%wide.region_13.14_spmd.clone, body=%wide.region_12.13_spmd.clone.sunk | while | flops 199688 | bytes 599253 | solution.py:32
  217.9 2.6 fusion.238
  223.0 2.6 fusion.238
  228.1 2.6 fusion.238
  232.8 6.5 fusion.74
  243.0 3.0 copy.169
  246.0 3.5 fusion.69
  252.0 3.5 reshape.1228
  255.4 3.1 multiply_convert_fusion.1
  263.6 3.8 copy.166
  267.4 3.7 reshape.1226
  271.2 2.6 fusion.91
  275.5 3.8 copy.153
  279.4 3.7 reshape.1222
  283.2 4.3 multiply_reduce_fusion.1
  296.7 5.3 fusion.184
  302.7 20.4 %multiply_convert_fusion = (bf16[512,3072]{1,0:T(8,128)(2,1)}, f32[512,3072]{1,0:T(8,128)S(1)}, f32[512,3072]{1,0:T(8,128)}) fusion(f32[3072]{0:T(1024)} %param.36, bf16[768,3072]{1,0:T(8,128)(2,1)} %param.35, bf16[1,512,768]{2,1,0:T(8,128)(2,1)} %param.22, f32[768]{0:T(1024)S(1)} %copy-done.78, f32[768]{0:T(1024)S(1)} %copy-done.70, f32[512]{0:T(512)S(1)} %fusion.162, ...), kind=kOutput, calls=%fused_computation.14 | convolution fusion | flops 2522087424 | bytes 21256192 | tf_op jit(solution)/shard_map/dot_general | solution.py:210
  323.1 8.6 convert_reduce_fusion
  333.3 5.5 fusion.187
  339.3 8.5 fusion.99
  347.9 38.5 %reduce-scatter.5.cloned.1.call-done = f32[96,2304]{1,0:T(8,128)} async-done(((f32[768,2304]{1,0:T(8,128)}), f32[96,2304]{1,0:T(8,128)}) %reduce-scatter.5.cloned.1.call-update) | async-done | bytes 884752 | tf_op jit(solution)/shard_map/reduce_scatter | solution.py:309
  386.3 100.8 %reduce-scatter.9.cloned.1.call-done = f32[96,3072]{1,0:T(8,128)} async-done(((f32[768,3072]{1,0:T(8,128)}), f32[96,3072]{1,0:T(8,128)}) %reduce-scatter.9.cloned.1.call-update) | async-done | bytes 1179664 | tf_op jit(solution)/shard_map/reduce_scatter | solution.py:311
  487.1 100.6 %reduce-scatter.11.cloned.1.call-done = f32[384,768]{1,0:T(8,128)} async-done(((f32[3072,768]{1,0:T(8,128)}), f32[384,768]{1,0:T(8,128)}) %reduce-scatter.11.cloned.1.call-update) | async-done | bytes 1179664 | tf_op jit(solution)/shard_map/reduce_scatter | solution.py:312
  587.8 98.1 %all-reduce.11.cloned.1.call-done = (f32[96,2304]{1,0:T(8,128)}, f32[96,768]{1,0:T(8,128)}, f32[96,3072]{1,0:T(8,128)}, f32[384,768]{1,0:T(8,128)}) async-done(((f32[96,2304]{1,0:T(8,128)}, f32[96,768]{1,0:T(8,128)}, f32[96,3072]{1,0:T(8,128)}, f32[384,768]{1,0:T(8,128)}), (f32[96,2304]{1,0:T(8,128)}, f32[96,768]{1,0:T(8,128)}, f32[96,3072]{1,0:T(8,128)}, ...) | async-done | bytes 3538960 | tf_op jit(solution)/shard_map/psum | solution.py:314
  688.2 4.4 fusion.202
  692.6 7.6 fusion.48
  705.8 2.6 convert_reduce_fusion.1
  708.4 3.2 fusion.46
  711.6 45.7 %all-reduce.7 = (f32[768]{0:T(1024)}, f32[768]{0:T(1024)}, f32[768]{0:T(1024)}, f32[768]{0:T(1024)}, f32[2304]{0:T(1024)}, /*index=5*/f32[12,64]{1,0:T(8,128)}, f32[768]{0:T(1024)}, f32[3072]{0:T(1024)}) all-reduce(f32[768]{0:T(1024)} %get-tuple-element.392, ...), channel_id=1, replica_groups=mesh['seq'=4,'batch'=8] {'seq','batch'}, use_global_device_ids=true, to_apply=%region_18.19 | all-reduce | flops 9984 | bytes 79872 | tf_op jit(solution)/shard_map/psum | solution.py:294
  758.7 6.0 fusion.203
  769.1 23.3 %all-gather.11.cloned.1.call-done = f32[768,2304]{1,0:T(8,128)} async-done(((f32[96,2304]{1,0:T(8,128)}), f32[768,2304]{1,0:T(8,128)}) %all-gather.11.cloned.1.call-update) | async-done | bytes 7077904 | tf_op jit(solution)/shard_map/all_gather | solution.py:316
  792.4 90.9 %all-gather.15.cloned.1.call-done = f32[768,3072]{1,0:T(8,128)} async-done(((f32[96,3072]{1,0:T(8,128)}), f32[768,3072]{1,0:T(8,128)}) %all-gather.15.cloned.1.call-update) | async-done | bytes 9437200 | tf_op jit(solution)/shard_map/all_gather | solution.py:318
  883.3 90.9 %all-gather.17.cloned.1.call-done = f32[3072,768]{1,0:T(8,128)} async-done(((f32[384,768]{1,0:T(8,128)}), f32[3072,768]{1,0:T(8,128)}) %all-gather.17.cloned.1.call-update) | async-done | bytes 9437200 | tf_op jit(solution)/shard_map/all_gather | solution.py:319
  975.4 7.2 copy.305
  985.3 3.7 copy.307
  989.0 8.0 copy.308
  (368 shorter events, 132.0 us)
Async XLA Ops:
  7.2 5.2 copy-start
  7.2 340.7 %reduce-scatter.7.cloned.1.call-start = ((), (), s32[]{:S(2)}) async-start(), calls=%async_computation.6 | async-start | bytes 2654208 | tf_op jit(solution)/shard_map/reduce_scatter | solution.py:310
  8.9 3.5 copy-start.15
  8.9 3.5 copy-start.95
  8.9 3.5 copy-start.113
  8.9 3.5 copy-start.115
  25.8 3.7 copy-start.27
  26.6 4.7 copy-start.29
  28.2 3.1 copy-start.46
  28.2 3.1 copy-start.48
  31.2 3.7 copy-start.9
  84.1 4.7 copy-start.103
  101.9 3.8 copy-start.3
  142.9 6.8 copy-start.73
  142.9 6.8 copy-start.6
  142.9 8.1 copy-start.35
  142.9 8.1 copy-start.43
  149.6 5.4 copy-start.41
  151.6 3.4 copy-start.71
  154.9 3.3 copy-start.81
  167.8 218.5 %reduce-scatter.5.cloned.1.call-start = ((), (), s32[]{:S(2)}) async-start(), calls=%async_computation.4 | async-start | bytes 7962624 | tf_op jit(solution)/shard_map/reduce_scatter | solution.py:309
  181.2 4.3 copy-start.2
  185.5 14.3 %copy-start.65 = (f32[8,12,64]{2,1,0:T(8,128)S(1)}, f32[8,12,64]{2,1,0:T(8,128)}, u32[]{:S(2)}) copy-start(f32[8,12,64]{2,1,0:T(8,128)} %copy-done.64) | copy-start | bytes 73732
  185.5 14.3 %copy-start.72 = (f32[8,12,1,64]{3,2,1,0:T(1,128)S(1)}, f32[8,12,1,64]{3,2,1,0:T(1,128)}, u32[]{:S(2)}) copy-start(f32[8,12,1,64]{3,2,1,0:T(1,128)} %copy-done.71) | copy-start | bytes 73732
  185.5 14.3 %copy-start.82 = (f32[8,64]{1,0:T(8,128)S(1)}, f32[8,64]{1,0:T(8,128)}, u32[]{:S(2)}) copy-start(f32[8,64]{1,0:T(8,128)} %copy-done.81) | copy-start | bytes 6148
  185.5 14.3 %copy-start.85 = (f32[8,64,12]{1,2,0:T(8,128)S(1)}, f32[8,64,12]{1,2,0:T(8,128)}, u32[]{:S(2)}) copy-start(f32[8,64,12]{1,2,0:T(8,128)} %get-tuple-element.445) | copy-start | bytes 73732
  185.5 15.0 %copy-start.36 = (bf16[8,64,12,64]{3,1,2,0:T(8,128)(2,1)S(1)}, bf16[8,64,12,64]{3,1,2,0:T(8,128)(2,1)}, u32[]{:S(2)}) copy-start(bf16[8,64,12,64]{3,1,2,0:T(8,128)(2,1)} %copy.126) | copy-start | bytes 2359300
  243.0 3.0 copy-start.87
  255.4 4.2 copy-start.8
  279.4 3.8 copy-start.80
  283.1 4.4 copy-start.24
  283.1 4.4 copy-start.25
  283.1 4.4 copy-start.30
  283.1 4.4 copy-start.47
  283.1 4.4 copy-start.49
  283.1 4.4 copy-start.63
  302.0 185.1 %reduce-scatter.9.cloned.1.call-start = ((), (), s32[]{:S(2)}) async-start(), calls=%async_computation.8 | async-start | bytes 10616832 | tf_op jit(solution)/shard_map/reduce_scatter | solution.py:311
  302.7 20.4 %copy-start.32 = (bf16[1,512,768]{2,1,0:T(8,128)(2,1)S(1)}, bf16[1,512,768]{2,1,0:T(8,128)(2,1)}, u32[]{:S(2)}) copy-start(bf16[1,512,768]{2,1,0:T(8,128)(2,1)} %param.39) | copy-start | bytes 2359300
  302.7 20.4 %copy-start.114 = (f32[3072]{0:T(1024)S(1)}, f32[3072]{0:T(1024)}, u32[]{:S(2)}) copy-start(f32[3072]{0:T(1024)} %param.36) | copy-start | bytes 36868
  323.1 10.2 %copy-start.17 = (bf16[1,512,768]{2,1,0:T(8,128)(2,1)S(1)}, bf16[1,512,768]{2,1,0:T(8,128)(2,1)}, u32[]{:S(2)}) copy-start(bf16[1,512,768]{2,1,0:T(8,128)(2,1)} %param.22) | copy-start | bytes 2359300
  338.8 248.9 %reduce-scatter.11.cloned.1.call-start = ((), (), s32[]{:S(2)}) async-start(), calls=%async_computation.10 | async-start | bytes 10616832 | tf_op jit(solution)/shard_map/reduce_scatter | solution.py:312
  347.8 338.1 %all-reduce.11.cloned.1.call-start = ((), (), s32[]{:S(2)}) async-start(), calls=%async_computation.12 | async-start | bytes 7077888 | tf_op jit(solution)/shard_map/psum | solution.py:314
  587.8 181.3 %all-gather.13.cloned.1.call-start = ((), (), s32[]{:S(2)}) async-start(), calls=%async_computation.7 | async-start | bytes 2654208 | tf_op jit(solution)/shard_map/all_gather | solution.py:317
  686.0 106.4 %all-gather.11.cloned.1.call-start = ((), (), s32[]{:S(2)}) async-start(), calls=%async_computation.5 | async-start | bytes 7962624 | tf_op jit(solution)/shard_map/all_gather | solution.py:316
  686.7 196.6 %all-gather.15.cloned.1.call-start = ((), (), s32[]{:S(2)}) async-start(), calls=%async_computation.9 | async-start | bytes 10616832 | tf_op jit(solution)/shard_map/all_gather | solution.py:318
  687.5 286.7 %all-gather.17.cloned.1.call-start = ((), (), s32[]{:S(2)}) async-start(), calls=%async_computation.11 | async-start | bytes 10616832 | tf_op jit(solution)/shard_map/all_gather | solution.py:319
  688.2 4.4 copy-start.18
  688.2 4.4 copy-start.56
  688.2 4.4 copy-start.97
  692.6 7.6 copy-start.37
  703.7 4.7 copy-start.94
  703.7 4.7 copy-start.106
  703.7 4.7 copy-start.107
  703.7 4.7 copy-start.19
  703.7 4.7 copy-start.21
  703.7 4.7 copy-start.98
  708.4 3.2 copy-start.91
  758.7 6.1 copy-start.20
  758.7 6.1 copy-start.60
  758.7 6.1 copy-start.112
  758.7 6.1 copy-start.117
  758.7 6.1 copy-start.118
  975.4 7.2 copy-start.61
  975.4 9.8 copy-start.31
  (65 other events, 110.7 us)
Sparse Core Ops, SparseCore 0:
  168.0 40.4 reduce-scatter.6
  302.1 84.1 reduce-scatter.4
  389.2 97.8 reduce-scatter.8
  489.8 97.8 reduce-scatter.10
  591.1 94.8 all-reduce.10
  687.4 32.0 all-gather.12
  721.1 71.1 all-gather.10
  794.0 89.2 all-gather.14
  884.9 89.1 all-gather.16
where the time goes:
time: 1010 us; the launch traced here: 1000 us
  waiting for transfers between devices  545 us (54%)
  matrix products  140 us (14%)
  local copies, waits for them, and re-layouts  128 us (13%)
  blocking collectives  98 us (10%)
  other arithmetic  75.1 us (7%)
  between operations  15.9 us (2%)
    reduce_scatter x1, waiting for transfers between devices, per_device(): lax.psum_scatter(matrices[2], 'batch', scatter_dimension=0, tiled=True)  101 us
    reduce_scatter x1, waiting for transfers between devices, per_device(): lax.psum_scatter(matrices[3], 'batch', scatter_dimension=0, tiled=True)  101 us
    psum x1, waiting for transfers between devices, per_device(): shares = lax.psum((shares[0], shares[1], shares[2], shares[3]), 'seq')  98.1 us
    all_gather x1, waiting for transfers between devices, per_device(): lax.all_gather(shares[2], 'batch', axis=0, tiled=True)  90.9 us
    all_gather x1, waiting for transfers between devices, per_device(): lax.all_gather(shares[3], 'batch', axis=0, tiled=True)  90.9 us
    psum x1, blocking collectives, per_device(): lax.psum((first_gain_grad, first_shift_grad, second_gain_grad, second_shi...  45.7 us
    unnamed x249, local copies, waits for them, and re-layouts  44.7 us
    all_gather x4, blocking collectives, carried_in(): everything = jax.tree.map(lambda part: lax.all_gather(part, axis), array)  42.5 us
  transfers between devices with their start and end apart: 9, of which 7 were waited for; matrix products, arithmetic and copies ran while one was open for 18% of the time, Pallas kernels for 0%

commit v1 on v0

--- a/solution.py
+++ b/solution.py
@@ -30,6 +30,93 @@
         return jax.tree.map(lambda a, b: jnp.where(reached, a, b), new, before)
 
     return lax.fori_loop(0, count, lap, start)
+
+
+AXES = ("seq", "batch")
+
+
+def bit_groups():
+    seqs, batches = lax.axis_size("seq"), lax.axis_size("batch")
+    seq_bits = [batches << k for k in range(seqs.bit_length() - 1)]
+    batch_bits = [1 << k for k in range(batches.bit_length() - 1)]
+    return batch_bits[:1], seq_bits, batch_bits[1:]
+
+
+def own_index():
+    return lax.axis_index("seq") * lax.axis_size("batch") + lax.axis_index("batch")
+
+
+def swap(array, bit):
+    count = lax.axis_size("seq") * lax.axis_size("batch")
+    return lax.ppermute(array, AXES, [(i, i ^ bit) for i in range(count)])
+
+
+def bit_value(bit):
+    return (own_index() & bit) // bit
+
+
+def exchange_sum(parts):
+    flat = jnp.concatenate([p.reshape(-1) for p in parts])
+    core, seqs, rest = bit_groups()
+    for bit in core + seqs + rest:
+        flat = flat + swap(flat, bit)
+    out, at = [], 0
+    for p in parts:
+        out.append(flat[at : at + p.size].reshape(p.shape))
+        at += p.size
+    return out
+
+
+def reduce_scatter_rows(array, start, pieces, order):
+    terms = [(array, start)]
+    left = pieces
+    for bit in order:
+        left //= 2
+        mine = bit_value(bit)
+
+        def cut(which):
+            got = [lax.dynamic_slice_in_dim(t, at + which * left, left, 0) for t, at in terms]
+            total = got[0]
+            for g in got[1:]:
+                total = total + g
+            return total
+
+        came = swap(cut(1 - mine), bit)
+        terms = [(t, at + mine * left) for t, at in terms] + [(came, 0)]
+    total = None
+    for t, at in terms:
+        g = lax.dynamic_slice_in_dim(t, at, left, 0)
+        total = g if total is None else total + g
+    return total
+
+
+def gather_rows(piece, order):
+    for bit in order[:0:-1]:
+        came = swap(piece, bit)
+        mine = bit_value(bit)
+        piece = jnp.where(
+            mine == 0,
+            jnp.concatenate([piece, came], axis=0),
+            jnp.concatenate([came, piece], axis=0),
+        )
+    return piece, swap(piece, order[0])
+
+
+def reduce_chunks(array):
+    core, seqs, rest = bit_groups()
+    orders = (core + seqs + rest, core + seqs[::-1] + rest, core + rest[:1] + seqs + rest[1:])
+    count = lax.axis_size("seq") * lax.axis_size("batch")
+    rows, columns = array.shape
+    cut = array.reshape(len(orders) * count, rows // (len(orders) * count), columns)
+    out = jnp.zeros_like(cut)
+    for k, order in enumerate(orders):
+        piece = reduce_scatter_rows(cut, k * count, count, order)
+        own, other = gather_rows(piece, order)
+        mine = bit_value(order[0])
+        half = count // 2
+        out = lax.dynamic_update_slice_in_dim(out, own, k * count + mine * half, 0)
+        out = lax.dynamic_update_slice_in_dim(out, other, k * count + (1 - mine) * half, 0)
+    return out.reshape(rows, columns)
 
 
 def layer_norm(values, gain, shift):
@@ -291,32 +378,27 @@
         )
     )
     tokens_grad = (cotangent.astype(f32) + d_inputs).astype(b16)
-    small = lax.psum(
-        (
-            first_gain_grad,
-            first_shift_grad,
-            second_gain_grad,
-            second_shift_grad,
-            input_bias_grad,
-            feature_weight_grad,
-            bias_total,
-            up_bias_grad,
-        ),
-        ("seq", "batch"),
-    )
-    matrices = (input_weight_grad, output_weight_grad, up_weight_grad, down_weight_grad)
-    shares = (
-        lax.psum_scatter(matrices[0], "batch", scatter_dimension=0, tiled=True),
-        lax.psum_scatter(matrices[1], "batch", scatter_dimension=0, tiled=True),
-        lax.psum_scatter(matrices[2], "batch", scatter_dimension=0, tiled=True),
-        lax.psum_scatter(matrices[3], "batch", scatter_dimension=0, tiled=True),
-    )
-    shares = lax.psum((shares[0], shares[1], shares[2], shares[3]), "seq")
+    small_parts = (
+        first_gain_grad,
+        first_shift_grad,
+        second_gain_grad,
+        second_shift_grad,
+        input_bias_grad,
+        feature_weight_grad,
+        bias_total,
+        up_bias_grad,
+    )
+    small = exchange_sum(small_parts)
+    attn_grad = jnp.concatenate([input_weight_grad, output_weight_grad], axis=1)
+    down_sum = reduce_chunks(down_weight_grad)
+    up_sum = reduce_chunks(up_weight_grad)
+    attn_sum = reduce_chunks(attn_grad)
+    width = input_weight.shape[1]
     summed = (
-        lax.all_gather(shares[0], "batch", axis=0, tiled=True),
-        lax.all_gather(shares[1], "batch", axis=0, tiled=True),
-        lax.all_gather(shares[2], "batch", axis=0, tiled=True),
-        lax.all_gather(shares[3], "batch", axis=0, tiled=True),
+        attn_sum[:, :width],
+        attn_sum[:, width:],
+        up_sum,
+        down_sum,
     )
     return (
         result.reshape(seq_count, length, model_width),

time: 1010 us -> 849 us (0.84)
  waiting for transfers between devices: 545 us -> 256 us
  starting transfers between devices: 0.76 us -> 92.1 us
  other arithmetic: 75.1 us -> 141 us
  blocking collectives: 98 us -> 51 us
  local copies, waits for them, and re-layouts: 128 us -> 149 us
  between operations: 15.9 us -> 3.78 us
    ppermute x0 -> x95, waiting for transfers between devices: none -> 256 us  [swap(): return lax.ppermute(array, AXES, [(i, i ^ bit) for i in range(count)])]
    reduce_scatter x4 -> x0, waiting for transfers between devices: 240 us -> none  [the longest x1 101 us: per_device(): lax.psum_scatter(matrices[2], 'batch', scatter_dimension=0, tiled=True)]
    all_gather x4 -> x0, waiting for transfers between devices: 205 us -> none  [the longest x1 90.9 us: per_device(): lax.all_gather(shares[2], 'batch', axis=0, tiled=True)]
    psum x1 -> x0, waiting for transfers between devices: 98.1 us -> none  [per_device(): shares = lax.psum((shares[0], shares[1], shares[2], shares[3]), 'seq')]
    ppermute x0 -> x95, starting transfers between devices: none -> 92.1 us  [swap(): return lax.ppermute(array, AXES, [(i, i ^ bit) for i in range(count)])]
    psum x1 -> x0, blocking collectives: 45.7 us -> none  [per_device(): lax.psum((first_gain_grad, first_shift_grad, second_gain_grad, second_shi...]
    add x0 -> x29, other arithmetic: none -> 35.5 us  [the longest x18 29 us: cut(): total = total + g]
    unnamed x249 -> x250, local copies, waits for them, and re-layouts: 44.7 us -> 22.1 us
  transfers between devices with their start and end apart: 9 -> 95, of which waited for: 7 -> 46; matrix products, arithmetic and copies ran while one was open for 18% -> 20% of each run, Pallas kernels for 0% -> 0%
where the time goes in v1:
time: 849 us; the launch traced here: 837 us
  waiting for transfers between devices  256 us (30%)
  local copies, waits for them, and re-layouts  149 us (18%)
  matrix products  144 us (17%)
  other arithmetic  141 us (17%)
  starting transfers between devices  92.1 us (11%)
  blocking collectives  51 us (6%)
    ppermute x95, waiting for transfers between devices, swap(): return lax.ppermute(array, AXES, [(i, i ^ bit) for i in range(count)])  256 us
    ppermute x95, starting transfers between devices, swap(): return lax.ppermute(array, AXES, [(i, i ^ bit) for i in range(count)])  92.1 us
    all_gather x4, blocking collectives, carried_in(): everything = jax.tree.map(lambda part: lax.all_gather(part, axis), array)  41.4 us
    select_n x16, other arithmetic, lap(): return jax.tree.map(lambda a, b: jnp.where(reached, a, b), new, before)  31.3 us
    add x18, other arithmetic, cut(): total = total + g  29 us
    unnamed x250, local copies, waits for them, and re-layouts  22.1 us
    dot_general x1, matrix products, per_device(): jnp.dot(second_low, up_weight, preferred_element_type=f32) + up_bias  18.1 us
  transfers between devices with their start and end apart: 95, of which 46 were waited for; matrix products, arithmetic and copies ran while one was open for 20% of the time, Pallas kernels for 0%

profile of v1, /device:TPU:1, one launch (start us, length us, event | category | flops | bytes accessed | tf_op | source)
XLA Modules:
  0.0 836.7 jit_solution(6365726077928231506)
XLA Ops:
  61.5 9.6 %all-reduce.6 = f32[4]{0:T(128)} all-reduce(f32[4]{0:T(128)} %bitcast_dynamic-update-slice_fusion), channel_id=1, replica_groups=mesh['seq'=4,'batch'=8] {'seq'}, use_global_device_ids=true, to_apply=%add.6 | all-reduce | flops 4 | bytes 32
  77.2 3.8 reshape.1308
  88.5 6.1 all-gather.4
  100.4 3.9 fusion.45
  104.4 14.7 %all-gather = f32[48,64,64]{2,1,0:T(8,128)} all-gather(f32[12,64,64]{2,1,0:T(8,128)S(1)} %bitcast.442), channel_id=2, replica_groups=mesh['seq'=4,'batch'=8] {'seq'}, dimensions={0}, use_global_device_ids=true | all-gather | bytes 983040 | tf_op jit(solution)/shard_map/all_gather | solution.py:19
  119.0 20.8 %while.34 = (s32[]{:T(128)}, f32[1,12,64,64]{3,2,1,0:T(8,128)}, f32[1,12,64]{2,1,0:T(8,128)S(1)}, s32[]{:T(128)}, f32[4,1,12,64,64]{4,3,2,1,0:T(8,128)}, /*index...) while((s32[]{:T(128)}, f32[1,12,64,64]{3,2,1,0:T(8,128)}, ...), condition=%wide.region_6.7_spmd.clone, body=%wide.region_5.6_spmd.clone.sunk | while | flops 199684 | bytes 599191 | solution.py:32
  141.9 6.7 add_convert_fusion.2
  168.5 4.3 fusion.41
  172.8 13.8 %all-gather.2 = f32[48,64,64]{2,1,0:T(8,128)} all-gather(f32[12,64,64]{2,1,0:T(8,128)S(1)} %bitcast.443), channel_id=4, replica_groups=mesh['seq'=4,'batch'=8] {'seq'}, dimensions={0}, use_global_device_ids=true | all-gather | bytes 983040 | tf_op jit(solution)/shard_map/all_gather | solution.py:19
  188.7 6.9 all-gather.5
  195.6 20.8 %while.35 = (s32[]{:T(128)}, f32[1,12,64,64]{3,2,1,0:T(8,128)}, f32[1,12,64]{2,1,0:T(8,128)S(1)}, s32[]{:T(128)}, f32[4,1,12,64,64]{4,3,2,1,0:T(8,128)}, /*index...) while((s32[]{:T(128)}, f32[1,12,64,64]{3,2,1,0:T(8,128)}, ...), condition=%wide.region_13.14_spmd.clone, body=%wide.region_12.13_spmd.clone.sunk | while | flops 199688 | bytes 599253 | solution.py:32
  218.5 6.5 fusion.96
  231.6 4.3 fusion.36
  236.0 3.8 copy.172
  239.8 4.1 reshape.1255
  243.9 4.0 fusion.29
  248.0 3.8 copy.159
  251.8 3.7 reshape.1251
  255.6 4.3 multiply_reduce_fusion.1
  275.8 3.8 copy.146
  290.4 5.3 fusion.209
  295.7 8.9 %maximum_bitcast_fusion = f32[96,8,3072]{2,1,0:T(8,128)} fusion(f32[768,768]{1,0:T(8,128)} %fusion.123, f32[768,2304]{1,0:T(8,128)} %fusion.209), kind=kLoop, calls=%fused_computation.12 | loop fusion | flops 2359296 | bytes 18874368 | tf_op jit(solution)/shard_map/reshape | solution.py:110
  304.6 4.8 constant_dynamic-slice_fusion.4
  309.4 9.9 %collective-permute-start.25 = (f32[16,8,3072]{2,1,0:T(8,128)}, f32[16,8,3072]{2,1,0:T(8,128)}, u32[]{:S(2)}, u32[]{:S(2)}) collective-permute-start(f32[16,8,3072]{2,1,0:T(8,128)} %get-tuple-element.487), channel_id=1, source_target_pairs={{0,1},{1,0},{2,3},{3,2},{4,5},{5,4},{6,7},{7,6},{8,9},{9,8},{10,11... | collective-permute-start | bytes 4718600 | tf_op jit(solution)/shard_map/ppermute | solution.py:51
  322.9 3.8 fusion.225
  326.8 18.1 %fusion.4 = (f32[512,3072]{1,0:T(8,128)S(1)}, f32[512,3072]{1,0:T(8,128)S(1)}) fusion(f32[3072]{0:T(1024)} %param.36, bf16[768,3072]{1,0:T(8,128)(2,1)} %param.35, f32[768]{0:T(1024)} %param.28, f32[768]{0:T(1024)} %param.27, f32[512]{0:T(512)S(1)} %copy-done.76, f32[512]{0:T(512)} %copy-done.82, bf16[1,512,768]{2,1,0:T(8,128)(2,1)} %param.22), kind=kOutput, calls=%fused_computation.13 | convolution fusion | flops 2517368832 | bytes 18110464 | tf_op jit(solution)/shard_map/dot_general | solution.py:297
  345.0 12.2 %convert_reduce_fusion = (f32[3072]{0:T(1024)S(1)}, bf16[512,3072]{1,0:T(8,128)(2,1)}) fusion(f32[512,3072]{1,0:T(8,128)S(1)} %get-tuple-element.534, bf16[3072,768]{1,0:T(8,128)(2,1)} %param.37, bf16[1,512,768]{2,1,0:T(8,128)(2,1)S(1)} %copy-done.28, f32[512,3072]{1,0:T(8,128)S(1)} %get-tuple-element.535, f32[3072]{0:T(1024)S(1)} %copy-done.96), kind=kOutput, calls=%fused_computation.34 | convolution fusion | flops 2442654720 | bytes 21258240 | tf_op jit(solution)/shard_map/td,fd->tf/dot_general | solution.py:306
  357.3 6.2 fusion.70
  370.2 4.5 fusion.30
  381.1 15.1 %fusion.7 = bf16[3072,512]{0,1:T(8,128)(2,1)S(1)} fusion(f32[512,3072]{1,0:T(8,128)} %copy-done.29, f32[3072]{0:T(1024)S(1)} %copy-done.96), kind=kLoop, calls=%fused_computation.16 | loop fusion | flops 103809024 | bytes 9449472 | tf_op jit(solution)/shard_map/convert_element_type | solution.py:299
  399.8 4.7 fusion.120
  414.1 3.7 dynamic-slice_add_fusion.3
  420.2 11.2 %collective-permute-done.26 = f32[8,8,3072]{2,1,0:T(8,128)S(1)} collective-permute-done((f32[8,8,3072]{2,1,0:T(8,128)S(1)}, f32[8,8,3072]{2,1,0:T(8,128)S(1)}, u32[]{:S(2)}, u32[]{:S(2)}) %collective-permute-start.26) | collective-permute-done | bytes 786464 | tf_op jit(solution)/shard_map/ppermute | solution.py:51
  437.3 11.1 %collective-permute-done.56 = f32[8,8,3072]{2,1,0:T(8,128)S(1)} collective-permute-done((f32[8,8,3072]{2,1,0:T(8,128)S(1)}, f32[8,8,3072]{2,1,0:T(8,128)S(1)}, u32[]{:S(2)}, u32[]{:S(2)}) %collective-permute-start.56) | collective-permute-done | bytes 786464 | tf_op jit(solution)/shard_map/ppermute | solution.py:51
  456.6 8.6 %collective-permute-done.86 = f32[8,32,768]{2,1,0:T(8,128)S(1)} collective-permute-done((f32[8,32,768]{2,1,0:T(8,128)S(1)}, f32[8,32,768]{2,1,0:T(8,128)S(1)}, u32[]{:S(2)}, u32[]{:S(2)}) %collective-permute-start.86) | collective-permute-done | bytes 786464 | tf_op jit(solution)/shard_map/ppermute | solution.py:51
  466.0 4.0 collective-permute-done.76
  473.5 5.2 collective-permute-done.27
  479.4 7.7 collective-permute-done.17
  491.0 4.5 collective-permute-done.57
  496.3 7.7 collective-permute-done.47
  512.6 8.2 collective-permute-done.77
  534.8 4.5 collective-permute-done.78
  548.6 7.4 collective-permute-done.39
  556.0 7.4 collective-permute-done.49
  570.8 6.3 collective-permute-done.79
  583.4 4.2 collective-permute-done.20
  587.6 6.3 collective-permute-done.10
  609.8 5.1 collective-permute-done.11
  619.2 4.2 collective-permute-done.41
  637.6 8.5 %collective-permute-done.12 = f32[4,8,3072]{2,1,0:T(8,128)S(1)} collective-permute-done((f32[4,8,3072]{2,1,0:T(8,128)S(1)}, f32[4,8,3072]{2,1,0:T(8,128)S(1)}, u32[]{:S(2)}, u32[]{:S(2)}) %collective-permute-start.12) | collective-permute-done | bytes 393248 | tf_op jit(solution)/shard_map/ppermute | solution.py:51
  647.9 7.4 collective-permute-done.42
  656.9 14.2 %collective-permute-done.13 = f32[8,8,3072]{2,1,0:T(8,128)S(1)} collective-permute-done((f32[8,8,3072]{2,1,0:T(8,128)S(1)}, f32[8,8,3072]{2,1,0:T(8,128)S(1)}, u32[]{:S(2)}, u32[]{:S(2)}) %collective-permute-start.13) | collective-permute-done | bytes 786464 | tf_op jit(solution)/shard_map/ppermute | solution.py:51
  673.3 5.7 collective-permute-done.72
  679.0 3.7 collective-permute-start.14
  682.8 13.7 %collective-permute-done.43 = f32[8,8,3072]{2,1,0:T(8,128)S(1)} collective-permute-done((f32[8,8,3072]{2,1,0:T(8,128)S(1)}, f32[8,8,3072]{2,1,0:T(8,128)S(1)}, u32[]{:S(2)}, u32[]{:S(2)}) %collective-permute-start.43) | collective-permute-done | bytes 786464 | tf_op jit(solution)/shard_map/ppermute | solution.py:51
  702.4 11.6 %collective-permute-done.73 = f32[8,32,768]{2,1,0:T(8,128)S(1)} collective-permute-done((f32[8,32,768]{2,1,0:T(8,128)S(1)}, f32[8,32,768]{2,1,0:T(8,128)S(1)}, u32[]{:S(2)}, u32[]{:S(2)}) %collective-permute-start.73) | collective-permute-done | bytes 786464 | tf_op jit(solution)/shard_map/ppermute | solution.py:51
  720.9 5.2 collective-permute-start.74
  733.8 8.6 %collective-permute-start.54 = (f32[16,8,3072]{2,1,0:T(8,128)S(1)}, f32[16,8,3072]{2,1,0:T(8,128)S(1)}, u32[]{:S(2)}, u32[]{:S(2)}) collective-permute-start(f32[16,8,3072]{2,1,0:T(8,128)S(1)} %get-tuple-element.432), channel_id=1, source_target_pairs={{0,1},{1,0},{2,3},{3,2},{4,5},{5,4},{6,7},{7,6},{8,9},{9,8},{10,11... | collective-permute-start | bytes 4718600 | tf_op jit(solution)/shard_map/ppermute | solution.py:51
  750.7 6.7 collective-permute-start.84
  758.9 4.0 collective-permute-done.33
  765.8 14.8 %collective-permute-done.63 = f32[8,8,3072]{2,1,0:T(8,128)S(1)} collective-permute-done((f32[8,8,3072]{2,1,0:T(8,128)S(1)}, f32[8,8,3072]{2,1,0:T(8,128)S(1)}, u32[]{:S(2)}, u32[]{:S(2)}) %collective-permute-start.63) | collective-permute-done | bytes 786464 | tf_op jit(solution)/shard_map/ppermute | solution.py:51
  783.5 13.9 %collective-permute-done.93 = f32[8,32,768]{2,1,0:T(8,128)S(1)} collective-permute-done((f32[8,32,768]{2,1,0:T(8,128)S(1)}, f32[8,32,768]{2,1,0:T(8,128)S(1)}, u32[]{:S(2)}, u32[]{:S(2)}) %collective-permute-start.93) | collective-permute-done | bytes 786464 | tf_op jit(solution)/shard_map/ppermute | solution.py:51
  799.9 10.2 %fusion.27 = f32[512,768]{1,0:T(8,128)S(1)} fusion(bf16[3072,768]{1,0:T(8,128)(2,1)} %param.37, f32[512,3072]{1,0:T(8,128)} %copy-done.115, f32[512,3072]{1,0:T(8,128)S(1)} %bitcast.422, f32[3072]{0:T(1024)S(1)} %copy-done.97), kind=kOutput, calls=%fused_computation.54 | convolution fusion | flops 2422210560 | bytes 18886656 | tf_op jit(solution)/shard_map/dot_general | solution.py:300
  823.9 6.4 slice.131
  (625 shorter events, 379.0 us)
Async XLA Ops:
  309.4 90.2 %collective-permute-start.25 = (f32[16,8,3072]{2,1,0:T(8,128)}, f32[16,8,3072]{2,1,0:T(8,128)}, u32[]{:S(2)}, u32[]{:S(2)}) collective-permute-start(f32[16,8,3072]{2,1,0:T(8,128)} %get-tuple-element.487), channel_id=1, source_target_pairs={{0,1},{1,0},{2,3},{3,2},{4,5},{5,4},{6,7},{7,6},{8,9},{9,8},{10,11... | collective-permute-start | bytes 4718600 | tf_op jit(solution)/shard_map/ppermute | solution.py:51
  319.3 89.2 %collective-permute-start.15 = (f32[16,8,3072]{2,1,0:T(8,128)}, f32[16,8,3072]{2,1,0:T(8,128)}, u32[]{:S(2)}, u32[]{:S(2)}) collective-permute-start(f32[16,8,3072]{2,1,0:T(8,128)} %get-tuple-element.488), channel_id=1, source_target_pairs={{0,1},{1,0},{2,3},{3,2},{4,5},{5,4},{6,7},{7,6},{8,9},{9,8},{10,11... | collective-permute-start | bytes 4718600 | tf_op jit(solution)/shard_map/ppermute | solution.py:51
  319.3 89.5 %collective-permute-start.5 = (f32[16,8,3072]{2,1,0:T(8,128)}, f32[16,8,3072]{2,1,0:T(8,128)}, u32[]{:S(2)}, u32[]{:S(2)}) collective-permute-start(f32[16,8,3072]{2,1,0:T(8,128)} %get-tuple-element.489), channel_id=1, source_target_pairs={{0,1},{1,0},{2,3},{3,2},{4,5},{5,4},{6,7},{7,6},{8,9},{9,8},{10,11... | collective-permute-start | bytes 4718600 | tf_op jit(solution)/shard_map/ppermute | solution.py:51
  379.9 29.2 %collective-permute-start.55 = (f32[16,8,3072]{2,1,0:T(8,128)}, f32[16,8,3072]{2,1,0:T(8,128)}, u32[]{:S(2)}, u32[]{:S(2)}) collective-permute-start(f32[16,8,3072]{2,1,0:T(8,128)} %get-tuple-element.472), channel_id=1, source_target_pairs={{0,1},{1,0},{2,3},{3,2},{4,5},{5,4},{6,7},{7,6},{8,9},{9,8},{10,11... | collective-permute-start | bytes 4718600 | tf_op jit(solution)/shard_map/ppermute | solution.py:51
  380.3 18.8 %collective-permute-start.1 = (f32[9984]{0:T(1024)S(1)}, f32[9984]{0:T(1024)S(1)}, u32[]{:S(2)}, u32[]{:S(2)}) collective-permute-start(f32[9984]{0:T(1024)S(1)} %add.1484), channel_id=1, source_target_pairs={{0,8},{1,9},{2,10},{3,11},{4,12},{5,13},{6,14},{7,15},{8,0},{9,1},... | collective-permute-start | bytes 119816 | tf_op jit(solution)/shard_map/ppermute | solution.py:51
  412.8 18.6 %collective-permute-start.26 = (f32[8,8,3072]{2,1,0:T(8,128)S(1)}, f32[8,8,3072]{2,1,0:T(8,128)S(1)}, u32[]{:S(2)}, u32[]{:S(2)}) collective-permute-start(f32[8,8,3072]{2,1,0:T(8,128)S(1)} %get-tuple-element.484), channel_id=1, source_target_pairs={{0,2},{1,3},{2,0},{3,1},{4,6},{5,7},{6,4},{7,5},{8,10},{9,11},{10,... | collective-permute-start | bytes 2359304 | tf_op jit(solution)/shard_map/ppermute | solution.py:51
  417.8 18.3 %collective-permute-start.16 = (f32[8,8,3072]{2,1,0:T(8,128)S(1)}, f32[8,8,3072]{2,1,0:T(8,128)S(1)}, u32[]{:S(2)}, u32[]{:S(2)}) collective-permute-start(f32[8,8,3072]{2,1,0:T(8,128)S(1)} %get-tuple-element.485), channel_id=1, source_target_pairs={{0,16},{1,17},{2,18},{3,19},{4,20},{5,21},{6,22},{7,23},{8,24},{9,... | collective-permute-start | bytes 2359304 | tf_op jit(solution)/shard_map/ppermute | solution.py:51
  418.5 18.0 %collective-permute-start.6 = (f32[8,8,3072]{2,1,0:T(8,128)S(1)}, f32[8,8,3072]{2,1,0:T(8,128)S(1)}, u32[]{:S(2)}, u32[]{:S(2)}) collective-permute-start(f32[8,8,3072]{2,1,0:T(8,128)S(1)} %get-tuple-element.486), channel_id=1, source_target_pairs={{0,8},{1,9},{2,10},{3,11},{4,12},{5,13},{6,14},{7,15},{8,0},{9,1},... | collective-permute-start | bytes 2359304 | tf_op jit(solution)/shard_map/ppermute | solution.py:51
  419.3 29.1 %collective-permute-start.56 = (f32[8,8,3072]{2,1,0:T(8,128)S(1)}, f32[8,8,3072]{2,1,0:T(8,128)S(1)}, u32[]{:S(2)}, u32[]{:S(2)}) collective-permute-start(f32[8,8,3072]{2,1,0:T(8,128)S(1)} %get-tuple-element.469), channel_id=1, source_target_pairs={{0,2},{1,3},{2,0},{3,1},{4,6},{5,7},{6,4},{7,5},{8,10},{9,11},{10,... | collective-permute-start | bytes 2359304 | tf_op jit(solution)/shard_map/ppermute | solution.py:51
  419.5 33.6 %collective-permute-start.46 = (f32[8,8,3072]{2,1,0:T(8,128)}, f32[8,8,3072]{2,1,0:T(8,128)}, u32[]{:S(2)}, u32[]{:S(2)}) collective-permute-start(f32[8,8,3072]{2,1,0:T(8,128)} %get-tuple-element.470), channel_id=1, source_target_pairs={{0,16},{1,17},{2,18},{3,19},{4,20},{5,21},{6,22},{7,23},{8,24},{9,... | collective-permute-start | bytes 2359304 | tf_op jit(solution)/shard_map/ppermute | solution.py:51
  431.4 22.4 %collective-permute-start.36 = (f32[8,8,3072]{2,1,0:T(8,128)}, f32[8,8,3072]{2,1,0:T(8,128)}, u32[]{:S(2)}, u32[]{:S(2)}) collective-permute-start(f32[8,8,3072]{2,1,0:T(8,128)} %get-tuple-element.471), channel_id=1, source_target_pairs={{0,8},{1,9},{2,10},{3,11},{4,12},{5,13},{6,14},{7,15},{8,0},{9,1},... | collective-permute-start | bytes 2359304 | tf_op jit(solution)/shard_map/ppermute | solution.py:51
  436.1 29.1 %collective-permute-start.86 = (f32[8,32,768]{2,1,0:T(8,128)S(1)}, f32[8,32,768]{2,1,0:T(8,128)S(1)}, u32[]{:S(2)}, u32[]{:S(2)}) collective-permute-start(f32[8,32,768]{2,1,0:T(8,128)S(1)} %get-tuple-element.454), channel_id=1, source_target_pairs={{0,2},{1,3},{2,0},{3,1},{4,6},{5,7},{6,4},{7,5},{8,10},{9,11},{10,... | collective-permute-start | bytes 2359304 | tf_op jit(solution)/shard_map/ppermute | solution.py:51
  436.5 33.4 %collective-permute-start.76 = (f32[8,32,768]{2,1,0:T(8,128)S(1)}, f32[8,32,768]{2,1,0:T(8,128)}, u32[]{:S(2)}, u32[]{:S(2)}) collective-permute-start(f32[8,32,768]{2,1,0:T(8,128)S(1)} %get-tuple-element.455), channel_id=1, source_target_pairs={{0,16},{1,17},{2,18},{3,19},{4,20},{5,21},{6,22},{7,23},{8,24},{9,... | collective-permute-start | bytes 2359304 | tf_op jit(solution)/shard_map/ppermute | solution.py:51
  449.3 21.4 %collective-permute-start.66 = (f32[8,32,768]{2,1,0:T(8,128)S(1)}, f32[8,32,768]{2,1,0:T(8,128)}, u32[]{:S(2)}, u32[]{:S(2)}) collective-permute-start(f32[8,32,768]{2,1,0:T(8,128)S(1)} %get-tuple-element.456), channel_id=1, source_target_pairs={{0,8},{1,9},{2,10},{3,11},{4,12},{5,13},{6,14},{7,15},{8,0},{9,1},... | collective-permute-start | bytes 2359304 | tf_op jit(solution)/shard_map/ppermute | solution.py:51
  453.1 25.6 %collective-permute-start.27 = (f32[4,8,3072]{2,1,0:T(8,128)S(1)}, f32[4,8,3072]{2,1,0:T(8,128)S(1)}, u32[]{:S(2)}, u32[]{:S(2)}) collective-permute-start(f32[4,8,3072]{2,1,0:T(8,128)S(1)} %get-tuple-element.481), channel_id=1, source_target_pairs={{0,8},{1,9},{2,10},{3,11},{4,12},{5,13},{6,14},{7,15},{8,0},{9,1},... | collective-permute-start | bytes 1179656 | tf_op jit(solution)/shard_map/ppermute | solution.py:51
  453.8 33.3 %collective-permute-start.17 = (f32[4,8,3072]{2,1,0:T(8,128)S(1)}, f32[4,8,3072]{2,1,0:T(8,128)S(1)}, u32[]{:S(2)}, u32[]{:S(2)}) collective-permute-start(f32[4,8,3072]{2,1,0:T(8,128)S(1)} %get-tuple-element.483), channel_id=1, source_target_pairs={{0,8},{1,9},{2,10},{3,11},{4,12},{5,13},{6,14},{7,15},{8,0},{9,1},... | collective-permute-start | bytes 1179656 | tf_op jit(solution)/shard_map/ppermute | solution.py:51
  465.3 23.9 %collective-permute-start.7 = (f32[4,8,3072]{2,1,0:T(8,128)S(1)}, f32[4,8,3072]{2,1,0:T(8,128)S(1)}, u32[]{:S(2)}, u32[]{:S(2)}) collective-permute-start(f32[4,8,3072]{2,1,0:T(8,128)S(1)} %get-tuple-element.482), channel_id=1, source_target_pairs={{0,16},{1,17},{2,18},{3,19},{4,20},{5,21},{6,22},{7,23},{8,24},{9,... | collective-permute-start | bytes 1179656 | tf_op jit(solution)/shard_map/ppermute | solution.py:51
  470.0 25.6 %collective-permute-start.57 = (f32[4,8,3072]{2,1,0:T(8,128)S(1)}, f32[4,8,3072]{2,1,0:T(8,128)S(1)}, u32[]{:S(2)}, u32[]{:S(2)}) collective-permute-start(f32[4,8,3072]{2,1,0:T(8,128)S(1)} %get-tuple-element.466), channel_id=1, source_target_pairs={{0,8},{1,9},{2,10},{3,11},{4,12},{5,13},{6,14},{7,15},{8,0},{9,1},... | collective-permute-start | bytes 1179656 | tf_op jit(solution)/shard_map/ppermute | solution.py:51
  470.7 34.8 %collective-permute-start.37 = (f32[4,8,3072]{2,1,0:T(8,128)S(1)}, f32[4,8,3072]{2,1,0:T(8,128)S(1)}, u32[]{:S(2)}, u32[]{:S(2)}) collective-permute-start(f32[4,8,3072]{2,1,0:T(8,128)S(1)} %get-tuple-element.467), channel_id=1, source_target_pairs={{0,16},{1,17},{2,18},{3,19},{4,20},{5,21},{6,22},{7,23},{8,24},{9,... | collective-permute-start | bytes 1179656 | tf_op jit(solution)/shard_map/ppermute | solution.py:51
  478.7 25.3 %collective-permute-start.47 = (f32[4,8,3072]{2,1,0:T(8,128)S(1)}, f32[4,8,3072]{2,1,0:T(8,128)S(1)}, u32[]{:S(2)}, u32[]{:S(2)}) collective-permute-start(f32[4,8,3072]{2,1,0:T(8,128)S(1)} %get-tuple-element.468), channel_id=1, source_target_pairs={{0,8},{1,9},{2,10},{3,11},{4,12},{5,13},{6,14},{7,15},{8,0},{9,1},... | collective-permute-start | bytes 1179656 | tf_op jit(solution)/shard_map/ppermute | solution.py:51
  487.1 25.3 %collective-permute-start.87 = (f32[4,32,768]{2,1,0:T(8,128)S(1)}, f32[4,32,768]{2,1,0:T(8,128)S(1)}, u32[]{:S(2)}, u32[]{:S(2)}) collective-permute-start(f32[4,32,768]{2,1,0:T(8,128)S(1)} %get-tuple-element.451), channel_id=1, source_target_pairs={{0,8},{1,9},{2,10},{3,11},{4,12},{5,13},{6,14},{7,15},{8,0},{9,1},... | collective-permute-start | bytes 1179656 | tf_op jit(solution)/shard_map/ppermute | solution.py:51
  489.2 18.3 %collective-permute-start.67 = (f32[4,32,768]{2,1,0:T(8,128)S(1)}, f32[4,32,768]{2,1,0:T(8,128)S(1)}, u32[]{:S(2)}, u32[]{:S(2)}) collective-permute-start(f32[4,32,768]{2,1,0:T(8,128)S(1)} %get-tuple-element.452), channel_id=1, source_target_pairs={{0,16},{1,17},{2,18},{3,19},{4,20},{5,21},{6,22},{7,23},{8,24},{9,... | collective-permute-start | bytes 1179656 | tf_op jit(solution)/shard_map/ppermute | solution.py:51
  495.5 25.3 %collective-permute-start.77 = (f32[4,32,768]{2,1,0:T(8,128)S(1)}, f32[4,32,768]{2,1,0:T(8,128)S(1)}, u32[]{:S(2)}, u32[]{:S(2)}) collective-permute-start(f32[4,32,768]{2,1,0:T(8,128)S(1)} %get-tuple-element.453), channel_id=1, source_target_pairs={{0,8},{1,9},{2,10},{3,11},{4,12},{5,13},{6,14},{7,15},{8,0},{9,1},... | collective-permute-start | bytes 1179656 | tf_op jit(solution)/shard_map/ppermute | solution.py:51
  503.9 21.6 %collective-permute-start.8 = (f32[2,8,3072]{2,1,0:T(8,128)S(1)}, f32[2,8,3072]{2,1,0:T(8,128)S(1)}, u32[]{:S(2)}, u32[]{:S(2)}) collective-permute-start(f32[2,8,3072]{2,1,0:T(8,128)S(1)} %dynamic-slice_add_fusion.26), channel_id=1, source_target_pairs={{0,2},{1,3},{2,0},{3,1},{4,6},{5,7},{6,4},{7,5},{8,10},{9,11},{10,... | collective-permute-start | bytes 589832 | tf_op jit(solution)/shard_map/ppermute | solution.py:51
  512.4 18.9 %collective-permute-start.38 = (f32[2,8,3072]{2,1,0:T(8,128)S(1)}, f32[2,8,3072]{2,1,0:T(8,128)S(1)}, u32[]{:S(2)}, u32[]{:S(2)}) collective-permute-start(f32[2,8,3072]{2,1,0:T(8,128)S(1)} %dynamic-slice_add_fusion.23), channel_id=1, source_target_pairs={{0,2},{1,3},{2,0},{3,1},{4,6},{5,7},{6,4},{7,5},{8,10},{9,11},{10,... | collective-permute-start | bytes 589832 | tf_op jit(solution)/shard_map/ppermute | solution.py:51
  540.5 24.1 %collective-permute-start.59 = (f32[1,8,3072]{2,1,0:T(8,128)S(1)}, f32[1,8,3072]{2,1,0:T(8,128)S(1)}, u32[]{:S(2)}, u32[]{:S(2)}) collective-permute-start(f32[1,8,3072]{2,1,0:T(8,128)S(1)} %get-tuple-element.462), channel_id=1, source_target_pairs={{0,4},{1,5},{2,6},{3,7},{4,0},{5,1},{6,2},{7,3},{8,12},{9,13},{10,... | collective-permute-start | bytes 294920 | tf_op jit(solution)/shard_map/ppermute | solution.py:51
  543.9 19.5 %collective-permute-start.49 = (f32[1,8,3072]{2,1,0:T(8,128)S(1)}, f32[1,8,3072]{2,1,0:T(8,128)S(1)}, u32[]{:S(2)}, u32[]{:S(2)}) collective-permute-start(f32[1,8,3072]{2,1,0:T(8,128)S(1)} %get-tuple-element.463), channel_id=1, source_target_pairs={{0,4},{1,5},{2,6},{3,7},{4,0},{5,1},{6,2},{7,3},{8,12},{9,13},{10,... | collective-permute-start | bytes 294920 | tf_op jit(solution)/shard_map/ppermute | solution.py:51
  544.0 26.7 %collective-permute-start.69 = (f32[1,32,768]{2,1,0:T(8,128)S(1)}, f32[1,32,768]{2,1,0:T(8,128)S(1)}, u32[]{:S(2)}, u32[]{:S(2)}) collective-permute-start(f32[1,32,768]{2,1,0:T(8,128)S(1)} %dynamic-slice_add_fusion.29), channel_id=1, source_target_pairs={{0,4},{1,5},{2,6},{3,7},{4,0},{5,1},{6,2},{7,3},{8,12},{9,13},{10,... | collective-permute-start | bytes 294920 | tf_op jit(solution)/shard_map/ppermute | solution.py:51
  547.5 30.8 %collective-permute-start.89 = (f32[1,32,768]{2,1,0:T(8,128)S(1)}, f32[1,32,768]{2,1,0:T(8,128)S(1)}, u32[]{:S(2)}, u32[]{:S(2)}) collective-permute-start(f32[1,32,768]{2,1,0:T(8,128)S(1)} %get-tuple-element.447), channel_id=1, source_target_pairs={{0,4},{1,5},{2,6},{3,7},{4,0},{5,1},{6,2},{7,3},{8,12},{9,13},{10,... | collective-permute-start | bytes 294920 | tf_op jit(solution)/shard_map/ppermute | solution.py:51
  556.0 21.1 %collective-permute-start.79 = (f32[1,32,768]{2,1,0:T(8,128)S(1)}, f32[1,32,768]{2,1,0:T(8,128)S(1)}, u32[]{:S(2)}, u32[]{:S(2)}) collective-permute-start(f32[1,32,768]{2,1,0:T(8,128)S(1)} %get-tuple-element.448), channel_id=1, source_target_pairs={{0,4},{1,5},{2,6},{3,7},{4,0},{5,1},{6,2},{7,3},{8,12},{9,13},{10,... | collective-permute-start | bytes 294920 | tf_op jit(solution)/shard_map/ppermute | solution.py:51
  563.4 20.0 %collective-permute-start.30 = (f32[1,8,3072]{2,1,0:T(8,128)S(1)}, f32[1,8,3072]{2,1,0:T(8,128)S(1)}, u32[]{:S(2)}, u32[]{:S(2)}) collective-permute-start(f32[1,8,3072]{2,1,0:T(8,128)S(1)} %add_add_fusion.8), channel_id=1, source_target_pairs={{0,4},{1,5},{2,6},{3,7},{4,0},{5,1},{6,2},{7,3},{8,12},{9,13},{10,... | collective-permute-start | bytes 294920 | tf_op jit(solution)/shard_map/ppermute | solution.py:51
  564.6 23.0 %collective-permute-start.20 = (f32[1,8,3072]{2,1,0:T(8,128)S(1)}, f32[1,8,3072]{2,1,0:T(8,128)S(1)}, u32[]{:S(2)}, u32[]{:S(2)}) collective-permute-start(f32[1,8,3072]{2,1,0:T(8,128)S(1)} %get-tuple-element.490), channel_id=1, source_target_pairs={{0,4},{1,5},{2,6},{3,7},{4,0},{5,1},{6,2},{7,3},{8,12},{9,13},{10,... | collective-permute-start | bytes 294920 | tf_op jit(solution)/shard_map/ppermute | solution.py:51
  570.8 23.2 %collective-permute-start.10 = (f32[1,8,3072]{2,1,0:T(8,128)S(1)}, f32[1,8,3072]{2,1,0:T(8,128)S(1)}, u32[]{:S(2)}, u32[]{:S(2)}) collective-permute-start(f32[1,8,3072]{2,1,0:T(8,128)S(1)} %get-tuple-element.491), channel_id=1, source_target_pairs={{0,4},{1,5},{2,6},{3,7},{4,0},{5,1},{6,2},{7,3},{8,12},{9,13},{10,... | collective-permute-start | bytes 294920 | tf_op jit(solution)/shard_map/ppermute | solution.py:51
  577.1 20.0 %collective-permute-start.60 = (f32[1,8,3072]{2,1,0:T(8,128)S(1)}, f32[1,8,3072]{2,1,0:T(8,128)S(1)}, u32[]{:S(2)}, u32[]{:S(2)}) collective-permute-start(f32[1,8,3072]{2,1,0:T(8,128)S(1)} %add_add_fusion.5), channel_id=1, source_target_pairs={{0,4},{1,5},{2,6},{3,7},{4,0},{5,1},{6,2},{7,3},{8,12},{9,13},{10,... | collective-permute-start | bytes 294920 | tf_op jit(solution)/shard_map/ppermute | solution.py:51
  578.3 22.0 %collective-permute-start.50 = (f32[1,8,3072]{2,1,0:T(8,128)S(1)}, f32[1,8,3072]{2,1,0:T(8,128)S(1)}, u32[]{:S(2)}, u32[]{:S(2)}) collective-permute-start(f32[1,8,3072]{2,1,0:T(8,128)S(1)} %get-tuple-element.475), channel_id=1, source_target_pairs={{0,4},{1,5},{2,6},{3,7},{4,0},{5,1},{6,2},{7,3},{8,12},{9,13},{10,... | collective-permute-start | bytes 294920 | tf_op jit(solution)/shard_map/ppermute | solution.py:51
  583.4 20.0 %collective-permute-start.40 = (f32[1,8,3072]{2,1,0:T(8,128)S(1)}, f32[1,8,3072]{2,1,0:T(8,128)S(1)}, u32[]{:S(2)}, u32[]{:S(2)}) collective-permute-start(f32[1,8,3072]{2,1,0:T(8,128)S(1)} %get-tuple-element.476), channel_id=1, source_target_pairs={{0,4},{1,5},{2,6},{3,7},{4,0},{5,1},{6,2},{7,3},{8,12},{9,13},{10,... | collective-permute-start | bytes 294920 | tf_op jit(solution)/shard_map/ppermute | solution.py:51
  587.6 18.0 %collective-permute-start.90 = (f32[1,32,768]{2,1,0:T(8,128)S(1)}, f32[1,32,768]{2,1,0:T(8,128)S(1)}, u32[]{:S(2)}, u32[]{:S(2)}) collective-permute-start(f32[1,32,768]{2,1,0:T(8,128)S(1)} %add_add_fusion.2), channel_id=1, source_target_pairs={{0,4},{1,5},{2,6},{3,7},{4,0},{5,1},{6,2},{7,3},{8,12},{9,13},{10,... | collective-permute-start | bytes 294920 | tf_op jit(solution)/shard_map/ppermute | solution.py:51
  605.6 17.8 %collective-permute-start.31 = (f32[2,8,3072]{2,1,0:T(8,128)S(1)}, f32[2,8,3072]{2,1,0:T(8,128)S(1)}, u32[]{:S(2)}, u32[]{:S(2)}) collective-permute-start(f32[2,8,3072]{2,1,0:T(8,128)S(1)} %maximum_select_fusion.29), channel_id=1, source_target_pairs={{0,16},{1,17},{2,18},{3,19},{4,20},{5,21},{6,22},{7,23},{8,24},{9,... | collective-permute-start | bytes 589832 | tf_op jit(solution)/shard_map/ppermute | solution.py:51
  609.8 17.8 %collective-permute-start.51 = (f32[2,8,3072]{2,1,0:T(8,128)S(1)}, f32[2,8,3072]{2,1,0:T(8,128)S(1)}, u32[]{:S(2)}, u32[]{:S(2)}) collective-permute-start(f32[2,8,3072]{2,1,0:T(8,128)S(1)} %maximum_select_fusion.31), channel_id=1, source_target_pairs={{0,2},{1,3},{2,0},{3,1},{4,6},{5,7},{6,4},{7,5},{8,10},{9,11},{10,... | collective-permute-start | bytes 589832 | tf_op jit(solution)/shard_map/ppermute | solution.py:51
  614.9 21.8 %collective-permute-start.61 = (f32[2,8,3072]{2,1,0:T(8,128)S(1)}, f32[2,8,3072]{2,1,0:T(8,128)S(1)}, u32[]{:S(2)}, u32[]{:S(2)}) collective-permute-start(f32[2,8,3072]{2,1,0:T(8,128)S(1)} %maximum_select_fusion.32), channel_id=1, source_target_pairs={{0,16},{1,17},{2,18},{3,19},{4,20},{5,21},{6,22},{7,23},{8,24},{9,... | collective-permute-start | bytes 589832 | tf_op jit(solution)/shard_map/ppermute | solution.py:51
  623.4 23.4 %collective-permute-start.91 = (f32[2,32,768]{2,1,0:T(8,128)S(1)}, f32[2,32,768]{2,1,0:T(8,128)S(1)}, u32[]{:S(2)}, u32[]{:S(2)}) collective-permute-start(f32[2,32,768]{2,1,0:T(8,128)S(1)} %maximum_select_fusion.35), channel_id=1, source_target_pairs={{0,16},{1,17},{2,18},{3,19},{4,20},{5,21},{6,22},{7,23},{8,24},{9,... | collective-permute-start | bytes 589832 | tf_op jit(solution)/shard_map/ppermute | solution.py:51
  627.5 28.5 %collective-permute-start.32 = (f32[4,8,3072]{2,1,0:T(8,128)S(1)}, f32[4,8,3072]{2,1,0:T(8,128)S(1)}, u32[]{:S(2)}, u32[]{:S(2)}) collective-permute-start(f32[4,8,3072]{2,1,0:T(8,128)S(1)} %maximum_select_fusion.20), channel_id=1, source_target_pairs={{0,8},{1,9},{2,10},{3,11},{4,12},{5,13},{6,14},{7,15},{8,0},{9,1},... | collective-permute-start | bytes 1179656 | tf_op jit(solution)/shard_map/ppermute | solution.py:51
  631.8 67.0 %collective-permute-start.22 = (f32[4,8,3072]{2,1,0:T(8,128)S(1)}, f32[4,8,3072]{2,1,0:T(8,128)S(1)}, u32[]{:S(2)}, u32[]{:S(2)}) collective-permute-start(f32[4,8,3072]{2,1,0:T(8,128)S(1)} %maximum_select_fusion.19), channel_id=1, source_target_pairs={{0,8},{1,9},{2,10},{3,11},{4,12},{5,13},{6,14},{7,15},{8,0},{9,1},... | collective-permute-start | bytes 1179656 | tf_op jit(solution)/shard_map/ppermute | solution.py:51
  636.7 64.0 %collective-permute-start.52 = (f32[4,8,3072]{2,1,0:T(8,128)S(1)}, f32[4,8,3072]{2,1,0:T(8,128)S(1)}, u32[]{:S(2)}, u32[]{:S(2)}) collective-permute-start(f32[4,8,3072]{2,1,0:T(8,128)S(1)} %maximum_select_fusion.22), channel_id=1, source_target_pairs={{0,8},{1,9},{2,10},{3,11},{4,12},{5,13},{6,14},{7,15},{8,0},{9,1},... | collective-permute-start | bytes 1179656 | tf_op jit(solution)/shard_map/ppermute | solution.py:51
  646.8 24.4 %collective-permute-start.13 = (f32[8,8,3072]{2,1,0:T(8,128)S(1)}, f32[8,8,3072]{2,1,0:T(8,128)S(1)}, u32[]{:S(2)}, u32[]{:S(2)}) collective-permute-start(f32[8,8,3072]{2,1,0:T(8,128)S(1)} %maximum_select_fusion.9), channel_id=1, source_target_pairs={{0,8},{1,9},{2,10},{3,11},{4,12},{5,13},{6,14},{7,15},{8,0},{9,1},... | collective-permute-start | bytes 2359304 | tf_op jit(solution)/shard_map/ppermute | solution.py:51
  655.3 46.3 %collective-permute-start.82 = (f32[4,32,768]{2,1,0:T(8,128)S(1)}, f32[4,32,768]{2,1,0:T(8,128)S(1)}, u32[]{:S(2)}, u32[]{:S(2)}) collective-permute-start(f32[4,32,768]{2,1,0:T(8,128)S(1)} %maximum_select_fusion.25), channel_id=1, source_target_pairs={{0,8},{1,9},{2,10},{3,11},{4,12},{5,13},{6,14},{7,15},{8,0},{9,1},... | collective-permute-start | bytes 1179656 | tf_op jit(solution)/shard_map/ppermute | solution.py:51
  656.1 40.4 %collective-permute-start.43 = (f32[8,8,3072]{2,1,0:T(8,128)S(1)}, f32[8,8,3072]{2,1,0:T(8,128)S(1)}, u32[]{:S(2)}, u32[]{:S(2)}) collective-permute-start(f32[8,8,3072]{2,1,0:T(8,128)S(1)} %maximum_select_fusion.12), channel_id=1, source_target_pairs={{0,8},{1,9},{2,10},{3,11},{4,12},{5,13},{6,14},{7,15},{8,0},{9,1},... | collective-permute-start | bytes 2359304 | tf_op jit(solution)/shard_map/ppermute | solution.py:51
  679.0 39.5 %collective-permute-start.14 = (f32[16,8,3072]{2,1,0:T(8,128)S(1)}, f32[16,8,3072]{2,1,0:T(8,128)}, u32[]{:S(2)}, u32[]{:S(2)}) collective-permute-start(f32[16,8,3072]{2,1,0:T(8,128)S(1)} %get-tuple-element.440), channel_id=1, source_target_pairs={{0,1},{1,0},{2,3},{3,2},{4,5},{5,4},{6,7},{7,6},{8,9},{9,8},{10,11... | collective-permute-start | bytes 4718600 | tf_op jit(solution)/shard_map/ppermute | solution.py:51
  696.5 17.5 %collective-permute-start.73 = (f32[8,32,768]{2,1,0:T(8,128)S(1)}, f32[8,32,768]{2,1,0:T(8,128)S(1)}, u32[]{:S(2)}, u32[]{:S(2)}) collective-permute-start(f32[8,32,768]{2,1,0:T(8,128)S(1)} %maximum_select_fusion.15), channel_id=1, source_target_pairs={{0,8},{1,9},{2,10},{3,11},{4,12},{5,13},{6,14},{7,15},{8,0},{9,1},... | collective-permute-start | bytes 2359304 | tf_op jit(solution)/shard_map/ppermute | solution.py:51
  698.7 29.1 %collective-permute-start.44 = (f32[16,8,3072]{2,1,0:T(8,128)S(1)}, f32[16,8,3072]{2,1,0:T(8,128)}, u32[]{:S(2)}, u32[]{:S(2)}) collective-permute-start(f32[16,8,3072]{2,1,0:T(8,128)S(1)} %get-tuple-element.434), channel_id=1, source_target_pairs={{0,1},{1,0},{2,3},{3,2},{4,5},{5,4},{6,7},{7,6},{8,9},{9,8},{10,11... | collective-permute-start | bytes 4718600 | tf_op jit(solution)/shard_map/ppermute | solution.py:51
  700.7 20.2 %collective-permute-start.23 = (f32[8,8,3072]{2,1,0:T(8,128)S(1)}, f32[8,8,3072]{2,1,0:T(8,128)}, u32[]{:S(2)}, u32[]{:S(2)}) collective-permute-start(f32[8,8,3072]{2,1,0:T(8,128)S(1)} %maximum_select_fusion.10), channel_id=1, source_target_pairs={{0,16},{1,17},{2,18},{3,19},{4,20},{5,21},{6,22},{7,23},{8,24},{9,... | collective-permute-start | bytes 2359304 | tf_op jit(solution)/shard_map/ppermute | solution.py:51
  701.6 32.2 %collective-permute-start.62 = (f32[4,8,3072]{2,1,0:T(8,128)S(1)}, f32[4,8,3072]{2,1,0:T(8,128)}, u32[]{:S(2)}, u32[]{:S(2)}) collective-permute-start(f32[4,8,3072]{2,1,0:T(8,128)S(1)} %maximum_select_fusion.23), channel_id=1, source_target_pairs={{0,8},{1,9},{2,10},{3,11},{4,12},{5,13},{6,14},{7,15},{8,0},{9,1},... | collective-permute-start | bytes 1179656 | tf_op jit(solution)/shard_map/ppermute | solution.py:51
  714.9 28.7 %collective-permute-start.92 = (f32[4,32,768]{2,1,0:T(8,128)S(1)}, f32[4,32,768]{2,1,0:T(8,128)S(1)}, u32[]{:S(2)}, u32[]{:S(2)}) collective-permute-start(f32[4,32,768]{2,1,0:T(8,128)S(1)} %maximum_select_fusion.26), channel_id=1, source_target_pairs={{0,8},{1,9},{2,10},{3,11},{4,12},{5,13},{6,14},{7,15},{8,0},{9,1},... | collective-permute-start | bytes 1179656 | tf_op jit(solution)/shard_map/ppermute | solution.py:51
  720.9 22.9 %collective-permute-start.74 = (f32[16,32,768]{2,1,0:T(8,128)S(1)}, f32[16,32,768]{2,1,0:T(8,128)S(1)}, u32[]{:S(2)}, u32[]{:S(2)}) collective-permute-start(f32[16,32,768]{2,1,0:T(8,128)S(1)} %get-tuple-element.428), channel_id=1, source_target_pairs={{0,1},{1,0},{2,3},{3,2},{4,5},{5,4},{6,7},{7,6},{8,9},{9,8},{10,11... | collective-permute-start | bytes 4718600 | tf_op jit(solution)/shard_map/ppermute | solution.py:51
  727.8 22.9 %collective-permute-start.24 = (f32[16,8,3072]{2,1,0:T(8,128)S(1)}, f32[16,8,3072]{2,1,0:T(8,128)}, u32[]{:S(2)}, u32[]{:S(2)}) collective-permute-start(f32[16,8,3072]{2,1,0:T(8,128)S(1)} %get-tuple-element.438), channel_id=1, source_target_pairs={{0,1},{1,0},{2,3},{3,2},{4,5},{5,4},{6,7},{7,6},{8,9},{9,8},{10,11... | collective-permute-start | bytes 4718600 | tf_op jit(solution)/shard_map/ppermute | solution.py:51
  733.8 30.8 %collective-permute-start.54 = (f32[16,8,3072]{2,1,0:T(8,128)S(1)}, f32[16,8,3072]{2,1,0:T(8,128)S(1)}, u32[]{:S(2)}, u32[]{:S(2)}) collective-permute-start(f32[16,8,3072]{2,1,0:T(8,128)S(1)} %get-tuple-element.432), channel_id=1, source_target_pairs={{0,1},{1,0},{2,3},{3,2},{4,5},{5,4},{6,7},{7,6},{8,9},{9,8},{10,11... | collective-permute-start | bytes 4718600 | tf_op jit(solution)/shard_map/ppermute | solution.py:51
  743.6 19.2 %collective-permute-start.33 = (f32[8,8,3072]{2,1,0:T(8,128)S(1)}, f32[8,8,3072]{2,1,0:T(8,128)S(1)}, u32[]{:S(2)}, u32[]{:S(2)}) collective-permute-start(f32[8,8,3072]{2,1,0:T(8,128)S(1)} %maximum_select_fusion.11), channel_id=1, source_target_pairs={{0,2},{1,3},{2,0},{3,1},{4,6},{5,7},{6,4},{7,5},{8,10},{9,11},{10,... | collective-permute-start | bytes 2359304 | tf_op jit(solution)/shard_map/ppermute | solution.py:51
  743.8 66.3 %collective-permute-start.3 = (f32[9984]{0:T(1024)S(1)}, f32[9984]{0:T(1024)S(1)}, u32[]{:S(2)}, u32[]{:S(2)}) collective-permute-start(f32[9984]{0:T(1024)S(1)} %add.1486), channel_id=1, source_target_pairs={{0,2},{1,3},{2,0},{3,1},{4,6},{5,7},{6,4},{7,5},{8,10},{9,11},{10,... | collective-permute-start | bytes 119816 | tf_op jit(solution)/shard_map/ppermute | solution.py:51
  748.9 31.7 %collective-permute-start.63 = (f32[8,8,3072]{2,1,0:T(8,128)S(1)}, f32[8,8,3072]{2,1,0:T(8,128)S(1)}, u32[]{:S(2)}, u32[]{:S(2)}) collective-permute-start(f32[8,8,3072]{2,1,0:T(8,128)S(1)} %maximum_select_fusion.14), channel_id=1, source_target_pairs={{0,2},{1,3},{2,0},{3,1},{4,6},{5,7},{6,4},{7,5},{8,10},{9,11},{10,... | collective-permute-start | bytes 2359304 | tf_op jit(solution)/shard_map/ppermute | solution.py:51
  750.7 32.6 %collective-permute-start.84 = (f32[16,32,768]{2,1,0:T(8,128)S(1)}, f32[16,32,768]{2,1,0:T(8,128)S(1)}, u32[]{:S(2)}, u32[]{:S(2)}) collective-permute-start(f32[16,32,768]{2,1,0:T(8,128)S(1)} %get-tuple-element.426), channel_id=1, source_target_pairs={{0,1},{1,0},{2,3},{3,2},{4,5},{5,4},{6,7},{7,6},{8,9},{9,8},{10,11... | collective-permute-start | bytes 4718600 | tf_op jit(solution)/shard_map/ppermute | solution.py:51
  762.9 34.6 %collective-permute-start.93 = (f32[8,32,768]{2,1,0:T(8,128)S(1)}, f32[8,32,768]{2,1,0:T(8,128)S(1)}, u32[]{:S(2)}, u32[]{:S(2)}) collective-permute-start(f32[8,32,768]{2,1,0:T(8,128)S(1)} %maximum_select_fusion.17), channel_id=1, source_target_pairs={{0,2},{1,3},{2,0},{3,1},{4,6},{5,7},{6,4},{7,5},{8,10},{9,11},{10,... | collective-permute-start | bytes 2359304 | tf_op jit(solution)/shard_map/ppermute | solution.py:51
  764.6 53.4 %collective-permute-start.34 = (f32[16,8,3072]{2,1,0:T(8,128)}, f32[16,8,3072]{2,1,0:T(8,128)}, u32[]{:S(2)}, u32[]{:S(2)}) collective-permute-start(f32[16,8,3072]{2,1,0:T(8,128)} %get-tuple-element.436), channel_id=1, source_target_pairs={{0,1},{1,0},{2,3},{3,2},{4,5},{5,4},{6,7},{7,6},{8,9},{9,8},{10,11... | collective-permute-start | bytes 4718600 | tf_op jit(solution)/shard_map/ppermute | solution.py:51
  782.1 48.2 %collective-permute-start.64 = (f32[16,8,3072]{2,1,0:T(8,128)}, f32[16,8,3072]{2,1,0:T(8,128)}, u32[]{:S(2)}, u32[]{:S(2)}) collective-permute-start(f32[16,8,3072]{2,1,0:T(8,128)} %get-tuple-element.430), channel_id=1, source_target_pairs={{0,1},{1,0},{2,3},{3,2},{4,5},{5,4},{6,7},{7,6},{8,9},{9,8},{10,11... | collective-permute-start | bytes 4718600 | tf_op jit(solution)/shard_map/ppermute | solution.py:51
  799.0 34.0 %collective-permute-start.94 = (f32[16,32,768]{2,1,0:T(8,128)}, f32[16,32,768]{2,1,0:T(8,128)}, u32[]{:S(2)}, u32[]{:S(2)}) collective-permute-start(f32[16,32,768]{2,1,0:T(8,128)} %get-tuple-element.424), channel_id=1, source_target_pairs={{0,1},{1,0},{2,3},{3,2},{4,5},{5,4},{6,7},{7,6},{8,9},{9,8},{10,11... | collective-permute-start | bytes 4718600 | tf_op jit(solution)/shard_map/ppermute | solution.py:51
  (150 other events, 1073.9 us)
